TPU v7x, 1024 devices: a whole 8x8x8 slice. The times are simulated.
1024 devices in a mesh: blk: 64 (over x, z_lo, core), grp: 16 (over y, z_hi).
Axes of the slice: x: 8, y: 8, z: 8 (z_hi: 2, z_lo: 4; z = z_hi * 4 + z_lo), core: 2. Of those that a mesh axis runs over, the one named last changes fastest.
Arguments:
- node_feats: float32 [131072, 256], P(('blk', 'grp')), may hold values from -6 to 6
- dest_block: int32 [1024, 24], P(('blk', 'grp')), may hold values from 0 to 63, as said below
- col_tile: int32 [1024, 24], P(('blk', 'grp')), may hold values from 0 to 15
- tile_count: int32 [1024], P(('blk', 'grp')), may hold values from 1 to 24, as said below
- edge_tiles: bfloat16 [1024, 24, 128, 128], P(('blk', 'grp')), as said below
- w_self: bfloat16 [256, 256], replicated, may hold values from -0.375 to 0.375
- w_agg: bfloat16 [256, 256], replicated, may hold values from -0.375 to 0.375
- in_bias: float32 [256], replicated, may hold values from -3 to 3
- w_out: bfloat16 [256, 256], replicated, may hold values from -0.375 to 0.375
- out_gain: float32 [256], replicated, may hold values from 0.5 to 2
- grad_out: float32 [131072, 256], P(('blk', 'grp')), may hold values from -6 to 6
Outputs:
- updated: float32 [131072, 256], P(('blk', 'grp'))
- grad_x: float32 [131072, 256], P(('blk', 'grp'))
- tile_grads: bfloat16 [1024, 24, 128, 128], P(('blk', 'grp'))
Inputs may be any that keep to these rules, and one draw needn't show every extreme that they name: dest_block[s,t] lies at most 3 steps from the shard's own block s // 16 on the closed loop of 64 blocks; within one shard's row the slots name pairwise different (dest_block, col_tile) pairs. `tile_count`: in every draw some shard has all 24 slots live. `edge_tiles`: most entries are zero.
All inputs are finite; a program needn't handle non-finite values.
Results may differ from a plain program's by a relative error of at most 0.01.
Values may be sent and summed in bfloat16 or wider, within the bound.
A program may use at most 32 MiB of HBM per device.

v0:
```python
import jax
import jax.numpy as jnp
from jax import lax
from jax.sharding import PartitionSpec as P

TILE = 128
HALO = 3


ln_eps = 1e-05


def passed_along(value, axis, steps):
    count = lax.axis_size(axis)
    pairs = [(source, (source + steps) % count) for source in range(count)]
    return lax.ppermute(value, axis, pairs)


def node_forward(node_feats, feat_bf, agg_bf, w_self, w_agg, in_bias, w_out, out_gain):
    pre_act = (
        jnp.dot(feat_bf, w_self, preferred_element_type=jnp.float32)
        + jnp.dot(agg_bf, w_agg, preferred_element_type=jnp.float32)
        + in_bias
    )
    hidden = jax.nn.silu(pre_act).astype(jnp.bfloat16)
    mixed = jnp.dot(hidden, w_out, preferred_element_type=jnp.float32)
    centred = mixed - jnp.mean(mixed, axis=-1, keepdims=True)
    variance = jnp.mean(centred * centred, axis=-1, keepdims=True)
    inv_std = lax.rsqrt(variance + ln_eps)
    normed = centred * inv_std
    return (node_feats + out_gain * normed, pre_act, normed, inv_std)


def node_backward(grad_out, pre_act, normed, inv_std, w_self, w_agg, w_out, out_gain):
    g_norm = grad_out * out_gain
    g_mixed = inv_std * (
        g_norm
        - jnp.mean(g_norm, axis=-1, keepdims=True)
        - normed * jnp.mean(g_norm * normed, axis=-1, keepdims=True)
    )
    g_mixed = g_mixed.astype(jnp.bfloat16)
    g_hidden = jnp.dot(g_mixed, w_out.T, preferred_element_type=jnp.float32)
    sigmoid_z = jax.nn.sigmoid(pre_act)
    g_pre = (g_hidden * sigmoid_z * (1.0 + pre_act * (1.0 - sigmoid_z))).astype(jnp.bfloat16)
    own_grad = jnp.dot(g_pre, w_self.T, preferred_element_type=jnp.float32)
    agg_grad = jnp.dot(g_pre, w_agg.T, preferred_element_type=jnp.float32).astype(jnp.bfloat16)
    return (own_grad, agg_grad)


def body(
    node_feats,
    dest_block,
    col_tile,
    tile_count,
    edge_tiles,
    w_self,
    w_agg,
    in_bias,
    w_out,
    out_gain,
    grad_out,
):
    top_precision = lax.Precision.HIGHEST
    blocks = lax.axis_size("blk")
    halo_reach = HALO
    span = 2 * halo_reach + 1
    offsets = list(range(-halo_reach, 0)) + list(range(1, halo_reach + 1))
    row_count = node_feats.shape[0]
    feat_width = node_feats.shape[1]
    feat_bf = node_feats.astype(jnp.bfloat16)
    gathered = lax.all_gather(feat_bf, "grp", axis=0, tiled=True)
    col_tiles = gathered.shape[0] // TILE
    slot_count = dest_block.shape[1]
    targets = dest_block[0]
    columns = col_tile[0]
    live_slot = jnp.arange(slot_count) < tile_count[0]
    edge_weights = jnp.where(live_slot[:, None, None], edge_tiles[0], jnp.zeros((), jnp.bfloat16))
    column_features = gathered.reshape(col_tiles, TILE, feat_width)[columns]
    weighted_products = jnp.einsum(
        "jcx,jxv->jcv", edge_weights, column_features, preferred_element_type=jnp.float32
    )
    relative = (targets - lax.axis_index("blk") + halo_reach) % blocks
    near_hot = (jnp.arange(span)[:, None] == relative[None, :]).astype(jnp.float32)
    partial_value = jnp.dot(
        near_hot,
        weighted_products.reshape(slot_count, row_count * feat_width),
        precision=top_precision,
        preferred_element_type=jnp.float32,
    )
    partial_value = partial_value.reshape(span, row_count, feat_width)
    aggregate = partial_value[halo_reach]
    for offset in offsets:
        aggregate = aggregate + passed_along(partial_value[halo_reach + offset], "blk", offset)
    agg_bf = aggregate.astype(jnp.bfloat16)
    updated, pre_act, normed, inv_std = node_forward(
        node_feats, feat_bf, agg_bf, w_self, w_agg, in_bias, w_out, out_gain
    )
    own_grad, agg_grad = node_backward(
        grad_out, pre_act, normed, inv_std, w_self, w_agg, w_out, out_gain
    )
    received = {0: agg_grad}
    for offset in offsets:
        received[offset] = passed_along(agg_grad, "blk", -offset)
    near_stack = jnp.stack([received[offset] for offset in range(-halo_reach, halo_reach + 1)])
    target_gradients = near_stack[relative]
    selected_slots = jnp.einsum(
        "lme,lae->lma", target_gradients, column_features, preferred_element_type=jnp.float32
    )
    tile_message_terms = jnp.einsum(
        "ghx,ghv->gxv", edge_weights, target_gradients, preferred_element_type=jnp.float32
    )
    flat_terms = tile_message_terms.reshape(slot_count, TILE * feat_width)
    tile_grads = jnp.where(live_slot[:, None, None], selected_slots, 0.0).astype(jnp.bfloat16)[None]
    tiles_in = lax.axis_size("grp") * row_count // TILE
    col_hot = (jnp.arange(tiles_in)[:, None] == columns[None, :]).astype(jnp.float32)
    rows_sum = jnp.dot(
        col_hot, flat_terms, precision=top_precision, preferred_element_type=jnp.float32
    )
    shared = lax.psum_scatter(
        rows_sum.reshape(lax.axis_size("grp") * row_count, feat_width).astype(jnp.bfloat16),
        "grp",
        scatter_dimension=0,
        tiled=True,
    ).astype(jnp.float32)
    grad_x = grad_out + own_grad + shared
    return (updated, grad_x, tile_grads)


def solution(mesh):
    placed = (
        P(("blk", "grp"), None),
        P(("blk", "grp"), None),
        P(("blk", "grp"), None),
        P(("blk", "grp")),
        P(("blk", "grp"), None, None, None),
        P(),
        P(),
        P(),
        P(),
        P(),
        P(("blk", "grp"), None),
    )
    return jax.shard_map(
        body,
        mesh=mesh,
        in_specs=placed,
        out_specs=(
            P(("blk", "grp"), None),
            P(("blk", "grp"), None),
            P(("blk", "grp"), None, None, None),
        ),
        check_vma=False,
    )
```

profile of v0, /device:TPU:1, one launch (start us, length us, event | category | flops | bytes accessed | tf_op | source)
XLA Modules:
  0.0 430.2 jit_solution(15379804259218641976)
XLA Ops:
  7.2 1.6 convert_element_type.32
  9.5 0.7 fusion.18
  10.2 0.7 fusion.15
  10.9 110.1 %all-gather.2.cloned.1.call-done = bf16[2048,256]{1,0:T(8,128)(2,1)} async-done(((bf16[128,256]{1,0:T(8,128)(2,1)}), bf16[2048,256]{1,0:T(8,128)(2,1)}) %all-gather.2.cloned.1.call-update) | async-done | bytes 1048592 | tf_op jit(solution)/shard_map/all_gather | solution.py:71
  121.0 1.9 gather_fusion
  122.9 0.6 fusion.4
  123.6 1.8 copy.16
  125.4 1.1 fusion.13
  126.6 2.4 slice_reduce_fusion.5
  129.0 4.1 collective-permute-start.1
  133.4 0.7 squeeze.40
  134.1 0.7 squeeze.39
  134.8 0.7 squeeze.38
  135.5 0.7 squeeze.37
  136.1 6.5 %collective-permute-start.2 = (f32[128,256]{1,0:T(8,128)}, f32[128,256]{1,0:T(8,128)S(1)}, u32[]{:S(2)}, u32[]{:S(2)}) collective-permute-start(f32[128,256]{1,0:T(8,128)} %squeeze.37), channel_id=1, source_target_pairs={{0,1008},{16,0},{32,16},{48,32},{64,48},{80,64},{96,80},{112,96},{... | collective-permute-start | bytes 393224 | tf_op jit(solution)/shard_map/ppermute | solution.py:16
  142.6 1.9 collective-permute-start.3
  144.5 2.6 collective-permute-start.4
  147.2 2.1 collective-permute-start.5
  149.3 7.3 %collective-permute-start = (f32[128,256]{1,0:T(8,128)S(1)}, f32[128,256]{1,0:T(8,128)S(1)}, u32[]{:S(2)}, u32[]{:S(2)}) collective-permute-start(f32[128,256]{1,0:T(8,128)S(1)} %squeeze.35), channel_id=1, source_target_pairs={{0,976},{16,992},{32,1008},{48,0},{64,16},{80,32},{96,48},{112,64}... | collective-permute-start | bytes 393224 | tf_op jit(solution)/shard_map/ppermute | solution.py:16
  156.8 3.4 collective-permute-done.5
  160.1 4.1 collective-permute-done
  164.2 0.2 fusion.1
  164.4 0.3 fusion.23
  164.9 0.8 multiply_reduce_fusion.2
  165.7 0.3 multiply_convert_fusion
  165.9 0.2 convolution_convert_fusion.1
  166.1 1.9 collective-permute-start.6
  168.1 7.5 %collective-permute-start.11 = (bf16[128,256]{1,0:T(8,128)(2,1)S(1)}, bf16[128,256]{1,0:T(8,128)(2,1)S(1)}, u32[]{:S(2)}, u32[]{:S(2)}) collective-permute-start(bf16[128,256]{1,0:T(8,128)(2,1)S(1)} %convolution_convert_fusion.1), channel_id=1, source_target_pairs={{0,976},{16,992},{32,1008},{48,0},{64,16},{80,32},{96,48},{112,64}... | collective-permute-start | bytes 196616 | tf_op jit(solution)/shard_map/ppermute | solution.py:16
  175.6 1.9 collective-permute-start.10
  177.6 2.3 collective-permute-start.9
  179.9 3.3 collective-permute-start.8
  183.2 3.5 collective-permute-start.7
  186.7 0.6 bitcast_dynamic-update-slice_fusion.6
  187.3 5.1 %collective-permute-done.7 = bf16[128,256]{1,0:T(8,128)(2,1)S(1)} collective-permute-done((bf16[128,256]{1,0:T(8,128)(2,1)S(1)}, bf16[128,256]{1,0:T(8,128)(2,1)S(1)}, u32[]{:S(2)}, u32[]{:S(2)}) %collective-permute-start.7) | collective-permute-done | bytes 65568 | tf_op jit(solution)/shard_map/ppermute | solution.py:16
  192.4 0.6 bitcast_dynamic-update-slice_fusion.5
  193.0 0.6 bitcast_dynamic-update-slice_fusion.4
  193.7 0.6 bitcast_dynamic-update-slice_fusion.3
  194.3 0.6 bitcast_dynamic-update-slice_fusion.2
  195.0 0.6 bitcast_dynamic-update-slice_fusion.1
  195.6 0.6 bitcast_dynamic-update-slice_fusion
  196.2 1.7 gather_fusion.1
  197.9 2.1 fusion.3
  200.0 1.8 copy.17
  201.8 2.4 convolution_convert_fusion
  204.2 2.3 convert_element_type.39
  206.5 1.5 fusion
  208.0 213.6 %reduce-scatter.2.cloned.1.call-done = bf16[128,256]{1,0:T(8,128)(2,1)} async-done(((bf16[2048,256]{1,0:T(8,128)(2,1)}), bf16[128,256]{1,0:T(8,128)(2,1)}) %reduce-scatter.2.cloned.1.call-update) | async-done | bytes 65552 | tf_op jit(solution)/shard_map/reduce_scatter | solution.py:119
  421.6 1.7 fusion.2
  (49 shorter events, 0.7 us)
Async XLA Ops:
  7.2 157.2 %copy-start = (bf16[256,256]{1,0:T(8,128)(2,1)S(1)}, bf16[256,256]{1,0:T(8,128)(2,1)}, u32[]{:S(2)}) copy-start(bf16[256,256]{1,0:T(8,128)(2,1)} %param.19) | copy-start | bytes 393220
  7.2 113.8 %all-gather.2.cloned.1.call-start = ((), (), s32[]{:S(2)}) async-start(), calls=%async_computation.1 | async-start | bytes 1114112 | tf_op jit(solution)/shard_map/all_gather | solution.py:71
  8.8 412.8 %reduce-scatter.2.cloned.1.call-start = ((), (), s32[]{:S(2)}) async-start(), calls=%async_computation.2 | async-start | bytes 1114112 | tf_op jit(solution)/shard_map/reduce_scatter | solution.py:119
  121.0 2.0 copy-start.1
  126.5 6.6 %copy-start.2 = (bf16[128,256]{1,0:T(8,128)(2,1)S(1)}, bf16[128,256]{1,0:T(8,128)(2,1)}, u32[]{:S(2)}) copy-start(bf16[128,256]{1,0:T(8,128)(2,1)} %convert_element_type.32) | copy-start | bytes 196612
  126.6 6.6 %copy-start.5 = (bf16[256,256]{1,0:T(8,128)(2,1)S(1)}, bf16[256,256]{1,0:T(8,128)(2,1)}, u32[]{:S(2)}) copy-start(bf16[256,256]{1,0:T(8,128)(2,1)} %param.16) | copy-start | bytes 393220
  126.6 30.1 %copy-start.11 = (s32[1,24]{1,0:T(1,128)S(1)}, s32[1,24]{1,0:T(1,128)}, u32[]{:S(2)}) copy-start(s32[1,24]{1,0:T(1,128)} %param.12) | copy-start | bytes 292
  126.6 37.6 %copy-start.3 = (bf16[256,256]{1,0:T(8,128)(2,1)S(1)}, bf16[256,256]{1,0:T(8,128)(2,1)}, u32[]{:S(2)}) copy-start(bf16[256,256]{1,0:T(8,128)(2,1)} %param.17) | copy-start | bytes 393220
  126.6 37.6 %copy-start.9 = (f32[256]{0:T(256)S(1)}, f32[256]{0:T(256)}, u32[]{:S(2)}) copy-start(f32[256]{0:T(256)} %param.18) | copy-start | bytes 3076
  129.0 20.3 %collective-permute-start.1 = (f32[128,256]{1,0:T(8,128)S(1)}, f32[128,256]{1,0:T(8,128)S(1)}, u32[]{:S(2)}, u32[]{:S(2)}) collective-permute-start(f32[128,256]{1,0:T(8,128)S(1)} %squeeze.36), channel_id=1, source_target_pairs={{0,992},{16,1008},{32,0},{48,16},{64,32},{80,48},{96,64},{112,80},... | collective-permute-start | bytes 393224 | tf_op jit(solution)/shard_map/ppermute | solution.py:16
  134.1 30.8 %copy-start.4 = (f32[128,256]{1,0:T(8,128)S(1)}, f32[128,256]{1,0:T(8,128)}, u32[]{:S(2)}) copy-start(f32[128,256]{1,0:T(8,128)} %param.11) | copy-start | bytes 393220
  134.1 30.8 %copy-start.6 = (f32[128,256]{1,0:T(8,128)S(1)}, f32[128,256]{1,0:T(8,128)}, u32[]{:S(2)}) copy-start(f32[128,256]{1,0:T(8,128)} %param.21) | copy-start | bytes 393220
  134.1 30.8 %copy-start.8 = (f32[256]{0:T(256)S(1)}, f32[256]{0:T(256)}, u32[]{:S(2)}) copy-start(f32[256]{0:T(256)} %param.20) | copy-start | bytes 3076
  136.1 20.6 %collective-permute-start.2 = (f32[128,256]{1,0:T(8,128)}, f32[128,256]{1,0:T(8,128)S(1)}, u32[]{:S(2)}, u32[]{:S(2)}) collective-permute-start(f32[128,256]{1,0:T(8,128)} %squeeze.37), channel_id=1, source_target_pairs={{0,1008},{16,0},{32,16},{48,32},{64,48},{80,64},{96,80},{112,96},{... | collective-permute-start | bytes 393224 | tf_op jit(solution)/shard_map/ppermute | solution.py:16
  142.6 14.1 %collective-permute-start.3 = (f32[128,256]{1,0:T(8,128)}, f32[128,256]{1,0:T(8,128)S(1)}, u32[]{:S(2)}, u32[]{:S(2)}) collective-permute-start(f32[128,256]{1,0:T(8,128)} %squeeze.38), channel_id=1, source_target_pairs={{0,16},{16,32},{32,48},{48,64},{64,80},{80,96},{96,112},{112,128},... | collective-permute-start | bytes 393224 | tf_op jit(solution)/shard_map/ppermute | solution.py:16
  144.5 12.2 %collective-permute-start.4 = (f32[128,256]{1,0:T(8,128)}, f32[128,256]{1,0:T(8,128)S(1)}, u32[]{:S(2)}, u32[]{:S(2)}) collective-permute-start(f32[128,256]{1,0:T(8,128)} %squeeze.39), channel_id=1, source_target_pairs={{0,32},{16,48},{32,64},{48,80},{64,96},{80,112},{96,128},{112,144}... | collective-permute-start | bytes 393224 | tf_op jit(solution)/shard_map/ppermute | solution.py:16
  147.2 13.0 %collective-permute-start.5 = (f32[128,256]{1,0:T(8,128)}, f32[128,256]{1,0:T(8,128)S(1)}, u32[]{:S(2)}, u32[]{:S(2)}) collective-permute-start(f32[128,256]{1,0:T(8,128)} %squeeze.40), channel_id=1, source_target_pairs={{0,48},{16,64},{32,80},{48,96},{64,112},{80,128},{96,144},{112,160... | collective-permute-start | bytes 393224 | tf_op jit(solution)/shard_map/ppermute | solution.py:16
  149.3 14.9 %collective-permute-start = (f32[128,256]{1,0:T(8,128)S(1)}, f32[128,256]{1,0:T(8,128)S(1)}, u32[]{:S(2)}, u32[]{:S(2)}) collective-permute-start(f32[128,256]{1,0:T(8,128)S(1)} %squeeze.35), channel_id=1, source_target_pairs={{0,976},{16,992},{32,1008},{48,0},{64,16},{80,32},{96,48},{112,64}... | collective-permute-start | bytes 393224 | tf_op jit(solution)/shard_map/ppermute | solution.py:16
  165.9 29.7 %copy-start.7 = (bf16[128,256]{1,0:T(8,128)(2,1)}, bf16[128,256]{1,0:T(8,128)(2,1)S(1)}, u32[]{:S(2)}) copy-start(bf16[128,256]{1,0:T(8,128)(2,1)S(1)} %multiply_convert_fusion) | copy-start | bytes 196612
  166.1 17.0 %collective-permute-start.6 = (bf16[128,256]{1,0:T(8,128)(2,1)S(1)}, bf16[128,256]{1,0:T(8,128)(2,1)S(1)}, u32[]{:S(2)}, u32[]{:S(2)}) collective-permute-start(bf16[128,256]{1,0:T(8,128)(2,1)S(1)} %convolution_convert_fusion.1), channel_id=1, source_target_pairs={{0,48},{16,64},{32,80},{48,96},{64,112},{80,128},{96,144},{112,160... | collective-permute-start | bytes 196616 | tf_op jit(solution)/shard_map/ppermute | solution.py:16
  168.1 27.5 %collective-permute-start.11 = (bf16[128,256]{1,0:T(8,128)(2,1)S(1)}, bf16[128,256]{1,0:T(8,128)(2,1)S(1)}, u32[]{:S(2)}, u32[]{:S(2)}) collective-permute-start(bf16[128,256]{1,0:T(8,128)(2,1)S(1)} %convolution_convert_fusion.1), channel_id=1, source_target_pairs={{0,976},{16,992},{32,1008},{48,0},{64,16},{80,32},{96,48},{112,64}... | collective-permute-start | bytes 196616 | tf_op jit(solution)/shard_map/ppermute | solution.py:16
  175.6 19.3 %collective-permute-start.10 = (bf16[128,256]{1,0:T(8,128)(2,1)S(1)}, bf16[128,256]{1,0:T(8,128)(2,1)S(1)}, u32[]{:S(2)}, u32[]{:S(2)}) collective-permute-start(bf16[128,256]{1,0:T(8,128)(2,1)S(1)} %convolution_convert_fusion.1), channel_id=1, source_target_pairs={{0,992},{16,1008},{32,0},{48,16},{64,32},{80,48},{96,64},{112,80},... | collective-permute-start | bytes 196616 | tf_op jit(solution)/shard_map/ppermute | solution.py:16
  177.6 16.7 %collective-permute-start.9 = (bf16[128,256]{1,0:T(8,128)(2,1)S(1)}, bf16[128,256]{1,0:T(8,128)(2,1)S(1)}, u32[]{:S(2)}, u32[]{:S(2)}) collective-permute-start(bf16[128,256]{1,0:T(8,128)(2,1)S(1)} %convolution_convert_fusion.1), channel_id=1, source_target_pairs={{0,1008},{16,0},{32,16},{48,32},{64,48},{80,64},{96,80},{112,96},{... | collective-permute-start | bytes 196616 | tf_op jit(solution)/shard_map/ppermute | solution.py:16
  179.9 13.2 %collective-permute-start.8 = (bf16[128,256]{1,0:T(8,128)(2,1)S(1)}, bf16[128,256]{1,0:T(8,128)(2,1)S(1)}, u32[]{:S(2)}, u32[]{:S(2)}) collective-permute-start(bf16[128,256]{1,0:T(8,128)(2,1)S(1)} %convolution_convert_fusion.1), channel_id=1, source_target_pairs={{0,16},{16,32},{32,48},{48,64},{64,80},{80,96},{96,112},{112,128},... | collective-permute-start | bytes 196616 | tf_op jit(solution)/shard_map/ppermute | solution.py:16
  183.2 9.2 %collective-permute-start.7 = (bf16[128,256]{1,0:T(8,128)(2,1)S(1)}, bf16[128,256]{1,0:T(8,128)(2,1)S(1)}, u32[]{:S(2)}, u32[]{:S(2)}) collective-permute-start(bf16[128,256]{1,0:T(8,128)(2,1)S(1)} %convolution_convert_fusion.1), channel_id=1, source_target_pairs={{0,32},{16,48},{32,64},{48,80},{64,96},{80,112},{96,128},{112,144}... | collective-permute-start | bytes 196616 | tf_op jit(solution)/shard_map/ppermute | solution.py:16
  200.0 1.8 copy-start.10
Sparse Core Ops, SparseCore 0:
  13.0 107.9 all-gather.1
  206.7 214.8 reduce-scatter.1
where the time goes:
time: 435 us; the launch traced here: 430 us
  waiting for transfers between devices  336 us (77%)
  starting transfers between devices  45.2 us (10%)
  local copies, waits for them, and re-layouts  19.4 us (4%)
  between operations  15.1 us (3%)
  matrix products  10.4 us (2%)
    reduce_scatter x1, waiting for transfers between devices, body(): lax.psum_scatter(rows_sum.reshape(lax.axis_size('grp') * row_count, feat_...  214 us
    all_gather x1, waiting for transfers between devices, body(): gathered = lax.all_gather(feat_bf, 'grp', axis=0, tiled=True)  110 us
    ppermute x12, starting transfers between devices, passed_along(): return lax.ppermute(value, axis, pairs)  45.1 us
    ppermute x12, waiting for transfers between devices, passed_along(): return lax.ppermute(value, axis, pairs)  12.5 us
  transfers between devices with their start and end apart: 14, of which 5 were waited for; matrix products, arithmetic and copies ran while one was open for 2% of the time, Pallas kernels for 0%

commit v1 on v0

v1 whole, which is shorter than its diff:
```python
import jax
import jax.numpy as jnp
from jax import lax
from jax.experimental import pallas as pl
from jax.experimental.pallas import tpu as pltpu
from jax.sharding import PartitionSpec as P

HALO = 3
SPAN = 2 * HALO + 1
LN_EPS = 1e-05
BF16 = jnp.bfloat16
F32 = jnp.float32


def matmul(left, right):
    return jnp.dot(left, right, preferred_element_type=F32)


def matmul_nt(left, right):
    return lax.dot_general(left, right, (((1,), (1,)), ((), ())), preferred_element_type=F32)


def kernel(
    dest_ref,
    col_ref,
    count_ref,
    feats_hbm,
    edge_hbm,
    w_self_hbm,
    w_agg_hbm,
    bias_hbm,
    w_out_hbm,
    gain_hbm,
    grad_hbm,
    updated_hbm,
    grad_x_hbm,
    tile_grads_hbm,
    feats,
    edge,
    w_self,
    w_agg,
    bias,
    w_out,
    gain,
    grad,
    updated,
    grad_x,
    tile_grads,
    table_v,
    table,
    edge_t,
    dense,
    dense_t,
    gathered,
    part_out,
    part_in,
    near,
    red_out,
    red_in,
    swap_out,
    swap_in,
    pre_base,
    own_grad,
    local_sems,
    out_sems,
    table_sem,
    ring_send,
    ring_recv,
    pair_send,
    pair_recv,
    part_send,
    part_recv,
    near_send,
    near_recv,
    red_send,
    red_recv,
    swap_send,
    swap_recv,
):
    rows = feats.shape[0]
    half = feats.shape[1] // 2
    slots = edge.shape[0] - 1
    members = gathered.shape[1]
    ring = members // 2
    reach = ring // 2
    blocks = lax.axis_size("blk")
    blk = lax.axis_index("blk")
    grp = lax.axis_index("grp")
    ring_at = grp // 2
    plane = grp % 2

    def member(ring_pos, q):
        return lax.rem(ring_pos + 2 * ring, ring) * 2 + (plane if q == 0 else 1 - plane)

    def to_ring(direction):
        return {"grp": member(ring_at + (1 if direction == 0 else -1), 0)}

    def to_pair():
        return {"grp": member(ring_at, 1)}

    def to_blk(offset):
        return {"blk": lax.rem(blk + offset + blocks, blocks)}

    offsets = [o for o in range(-HALO, HALO + 1) if o != 0]

    loads = [
        pltpu.make_async_copy(src, dst, local_sems.at[i])
        for i, (src, dst) in enumerate(
            [
                (feats_hbm, feats),
                (edge_hbm.at[0], edge.at[pl.ds(0, slots)]),
                (w_self_hbm, w_self),
                (bias_hbm, bias),
                (w_agg_hbm, w_agg),
                (w_out_hbm, w_out),
                (gain_hbm, gain),
                (grad_hbm, grad),
            ]
        )
    ]
    for load in loads:
        load.start()

    barrier = pltpu.get_barrier_semaphore()
    greeted = [to_ring(0), to_ring(1), to_pair()] + [to_blk(o) for o in offsets]
    for target in greeted:
        pl.semaphore_signal(barrier, inc=1, device_id=target, device_id_type=pl.DeviceIdType.MESH)

    lane = lax.broadcasted_iota(jnp.int32, table_v.shape, 1)
    found = jnp.full(table_v.shape, slots, jnp.int32)
    for t in range(slots):
        rel = lax.rem(dest_ref[0, t] - blk + HALO + blocks, blocks)
        key = jnp.where(t < count_ref[0], rel * members + col_ref[0, t], -1)
        found = jnp.where(lane == key, t, found)
    table_v[...] = found
    table_copy = pltpu.make_async_copy(table_v, table, table_sem)
    table_copy.start()

    loads[0].wait()
    feat_bf = feats[...].astype(BF16)
    mine = member(ring_at, 0)
    for h in range(2):
        gathered[h, mine] = feat_bf[:, h * half : (h + 1) * half]

    pl.semaphore_wait(barrier, len(greeted))

    def ring_id(h, q, direction, step):
        return ((h * 2 + q) * 2 + direction) * reach + step - 1

    def in_flow(q, direction, step):
        return step < reach or q == direction

    def ring_copy(h, q, direction, step, incoming=False):
        back = step if incoming else step - 1
        at = member(ring_at + (-back if direction == 0 else back), q)
        i = ring_id(h, q, direction, step)
        return pltpu.make_async_remote_copy(
            src_ref=gathered.at[h, at],
            dst_ref=gathered.at[h, at],
            send_sem=ring_send.at[i],
            recv_sem=ring_recv.at[i],
            device_id=to_ring(direction),
            device_id_type=pl.DeviceIdType.MESH,
        )

    def pair_copy(h, incoming=False):
        at = member(ring_at, 1 if incoming else 0)
        return pltpu.make_async_remote_copy(
            src_ref=gathered.at[h, at],
            dst_ref=gathered.at[h, at],
            send_sem=pair_send.at[h],
            recv_sem=pair_recv.at[h],
            device_id=to_pair(),
            device_id_type=pl.DeviceIdType.MESH,
        )

    def ring_step(h, q, step):
        for direction in range(2):
            if step > 1:
                ring_copy(h, q, direction, step - 1, incoming=True).wait_recv()
            if in_flow(q, direction, step):
                ring_copy(h, q, direction, step).start()

    for h in range(2):
        pair_copy(h).start()
        ring_step(h, 0, 1)

    loads[1].wait()
    edge[slots] = jnp.zeros((rows, rows), BF16)
    edge_t[slots] = jnp.zeros((rows, rows), BF16)
    table_copy.wait()

    def turn(t, carry):
        edge_t[t] = edge[t].T
        return carry

    def fill_dense(n, carry):
        for c in range(members):
            dense[n, :, c * rows : (c + 1) * rows] = edge[table[0, n * members + c]]
        return carry

    def fill_dense_t(c, carry):
        for n in range(SPAN):
            dense_t[c, :, n * rows : (n + 1) * rows] = edge_t[table[0, n * members + c]]
        return carry

    lax.fori_loop(0, SPAN, fill_dense, 0)
    for h in range(2):
        pair_copy(h, incoming=True).wait_recv()
        ring_step(h, 1, 1)
    for h in range(2):
        for q in range(2):
            ring_step(h, q, 2)
    lax.fori_loop(0, slots, turn, 0)
    for step in range(3, reach + 1):
        for h in range(2):
            for q in range(2):
                ring_step(h, q, step)

    def part_copy(h, offset):
        i = h * SPAN + offset + HALO
        return pltpu.make_async_remote_copy(
            src_ref=part_out.at[h, offset + HALO],
            dst_ref=part_in.at[h, offset + HALO],
            send_sem=part_send.at[i],
            recv_sem=part_recv.at[i],
            device_id=to_blk(offset),
            device_id_type=pl.DeviceIdType.MESH,
        )

    centre = []
    for h in range(2):
        for q in range(2):
            ring_copy(h, q, q, reach, incoming=True).wait_recv()
        columns = gathered[h].reshape(members * rows, half)
        for offset in sorted(offsets, key=lambda o: -abs(o)):
            part_out[h, offset + HALO] = matmul(dense[offset + HALO], columns).astype(BF16)
            part_copy(h, offset).start()
        centre.append(matmul(dense[HALO], columns))

    loads[2].wait()
    loads[3].wait()
    pre_base[...] = matmul(feat_bf, w_self[...]) + bias[...]
    lax.fori_loop(0, members, fill_dense_t, 0)
    for load in loads[4:]:
        load.wait()

    pre_act = pre_base[...]
    for h in range(2):
        total = centre[h]
        for offset in sorted(offsets, key=abs):
            part_copy(h, offset).wait_recv()
            total = total + part_in[h, offset + HALO].astype(F32)
        pre_act = pre_act + matmul(total.astype(BF16), w_agg[h * half : (h + 1) * half, :])
    sigmoid_z = jax.nn.sigmoid(pre_act)
    hidden = (pre_act * sigmoid_z).astype(BF16)
    mixed = matmul(hidden, w_out[...])
    centred = mixed - jnp.mean(mixed, axis=-1, keepdims=True)
    variance = jnp.mean(centred * centred, axis=-1, keepdims=True)
    inv_std = lax.rsqrt(variance + LN_EPS)
    normed = centred * inv_std

    g_norm = grad[...] * gain[...]
    g_mixed = inv_std * (
        g_norm
        - jnp.mean(g_norm, axis=-1, keepdims=True)
        - normed * jnp.mean(g_norm * normed, axis=-1, keepdims=True)
    )
    g_hidden = matmul_nt(g_mixed.astype(BF16), w_out[...])
    g_pre = (g_hidden * sigmoid_z * (1.0 + pre_act * (1.0 - sigmoid_z))).astype(BF16)

    def near_copy(h, offset):
        i = h * SPAN + offset + HALO
        return pltpu.make_async_remote_copy(
            src_ref=near.at[h, HALO],
            dst_ref=near.at[h, HALO - offset],
            send_sem=near_send.at[i],
            recv_sem=near_recv.at[i],
            device_id=to_blk(offset),
            device_id_type=pl.DeviceIdType.MESH,
        )

    for h in range(2):
        near[h, HALO] = matmul_nt(g_pre, w_agg[h * half : (h + 1) * half, :]).astype(BF16)
        for offset in sorted(offsets, key=lambda o: -abs(o)):
            near_copy(h, offset).start()

    updated[...] = feats[...] + gain[...] * normed
    stores = [pltpu.make_async_copy(updated, updated_hbm, out_sems.at[0])]
    stores[0].start()
    own_grad[...] = grad[...] + matmul_nt(g_pre, w_self[...])

    def red_copy(h, q, direction, step):
        i = ring_id(h, q, direction, step)
        return pltpu.make_async_remote_copy(
            src_ref=red_out.at[i],
            dst_ref=red_in.at[i],
            send_sem=red_send.at[i],
            recv_sem=red_recv.at[i],
            device_id=to_ring(direction),
            device_id_type=pl.DeviceIdType.MESH,
        )

    def red_flow(q, direction, step):
        return step > 1 or q == direction

    def message(h, ring_pos, q):
        return matmul(dense_t[member(ring_pos, q)], near[h].reshape(SPAN * rows, half))

    def red_step(h, step):
        distance = reach + 1 - step
        for q in (1, 0):
            for direction in range(2):
                if not red_flow(q, direction, step):
                    continue
                total = message(h, ring_at + (distance if direction == 0 else -distance), q)
                if step > 1 and red_flow(q, direction, step - 1):
                    red_copy(h, q, direction, step - 1).wait_recv()
                    total = total + red_in[ring_id(h, q, direction, step - 1)].astype(F32)
                red_out[ring_id(h, q, direction, step)] = total.astype(BF16)
                red_copy(h, q, direction, step).start()

    def swap_copy(h):
        return pltpu.make_async_remote_copy(
            src_ref=swap_out.at[h],
            dst_ref=swap_in.at[h],
            send_sem=swap_send.at[h],
            recv_sem=swap_recv.at[h],
            device_id=to_pair(),
            device_id_type=pl.DeviceIdType.MESH,
        )

    def red_total(h, q):
        total = message(h, ring_at, q)
        for direction in range(2):
            red_copy(h, q, direction, reach).wait_recv()
            total = total + red_in[ring_id(h, q, direction, reach)].astype(F32)
        return total

    def tile_gradient(t, carry):
        rel = jnp.clip(lax.rem(dest_ref[0, t] - blk + HALO + blocks, blocks), 0, SPAN - 1)
        col = jnp.clip(col_ref[0, t], 0, members - 1)
        value = matmul_nt(near[0, rel], gathered[0, col]) + matmul_nt(near[1, rel], gathered[1, col])
        tile_grads[t] = jnp.where(t < count_ref[0], value, 0.0).astype(BF16)
        return carry

    shares = reach
    share = slots // shares

    def tile_share(k):
        lax.fori_loop(k * share, (k + 1) * share, tile_gradient, 0)
        store = pltpu.make_async_copy(
            tile_grads.at[pl.ds(k * share, share)],
            tile_grads_hbm.at[0, pl.ds(k * share, share)],
            out_sems.at[2 + k],
        )
        store.start()
        stores.append(store)

    for h in range(2):
        for offset in sorted(offsets, key=abs):
            near_copy(h, offset).wait_recv()
        red_step(h, 1)
    for step in range(2, reach + 1):
        tile_share(step - 2)
        for h in range(2):
            red_step(h, step)
    tile_share(reach - 1)
    for h in range(2):
        swap_out[h] = red_total(h, 1).astype(BF16)
        swap_copy(h).start()
    own = [red_total(h, 0) for h in range(2)]
    for h in range(2):
        swap_copy(h).wait_recv()
        at = slice(h * half, (h + 1) * half)
        grad_x[:, at] = own_grad[:, at] + (own[h] + swap_in[h].astype(F32))
    stores.append(pltpu.make_async_copy(grad_x, grad_x_hbm, out_sems.at[1]))
    stores[-1].start()

    for h in range(2):
        pair_copy(h).wait_send()
        swap_copy(h).wait_send()
        for offset in offsets:
            part_copy(h, offset).wait_send()
            near_copy(h, offset).wait_send()
        for q in range(2):
            for direction in range(2):
                for step in range(1, reach + 1):
                    if in_flow(q, direction, step):
                        ring_copy(h, q, direction, step).wait_send()
                    if red_flow(q, direction, step):
                        red_copy(h, q, direction, step).wait_send()
    for store in stores:
        store.wait()


def body(
    node_feats,
    dest_block,
    col_tile,
    tile_count,
    edge_tiles,
    w_self,
    w_agg,
    in_bias,
    w_out,
    out_gain,
    grad_out,
):
    rows, feat = node_feats.shape
    half = feat // 2
    slots = dest_block.shape[1]
    members = lax.axis_size("grp")
    reach = members // 4
    flows = 8 * reach
    table_lanes = -(-SPAN * members // 128) * 128
    smem = pl.BlockSpec(memory_space=pltpu.SMEM)
    anywhere = pl.BlockSpec(memory_space=pl.ANY)
    dma = pltpu.SemaphoreType.DMA
    return pl.pallas_call(
        kernel,
        out_shape=(
            jax.ShapeDtypeStruct((rows, feat), F32),
            jax.ShapeDtypeStruct((rows, feat), F32),
            jax.ShapeDtypeStruct((1, slots, rows, rows), BF16),
        ),
        in_specs=[smem] * 3 + [anywhere] * 8,
        out_specs=[anywhere] * 3,
        scratch_shapes=[
            pltpu.VMEM((rows, feat), F32),
            pltpu.VMEM((slots + 1, rows, rows), BF16),
            pltpu.VMEM((feat, feat), BF16),
            pltpu.VMEM((feat, feat), BF16),
            pltpu.VMEM((1, feat), F32),
            pltpu.VMEM((feat, feat), BF16),
            pltpu.VMEM((1, feat), F32),
            pltpu.VMEM((rows, feat), F32),
            pltpu.VMEM((rows, feat), F32),
            pltpu.VMEM((rows, feat), F32),
            pltpu.VMEM((slots, rows, rows), BF16),
            pltpu.VMEM((1, table_lanes), jnp.int32),
            pltpu.SMEM((1, table_lanes), jnp.int32),
            pltpu.VMEM((slots + 1, rows, rows), BF16),
            pltpu.VMEM((SPAN, rows, members * rows), BF16),
            pltpu.VMEM((members, rows, SPAN * rows), BF16),
            pltpu.VMEM((2, members, rows, half), BF16),
            pltpu.VMEM((2, SPAN, rows, half), BF16),
            pltpu.VMEM((2, SPAN, rows, half), BF16),
            pltpu.VMEM((2, SPAN, rows, half), BF16),
            pltpu.VMEM((flows, rows, half), BF16),
            pltpu.VMEM((flows, rows, half), BF16),
            pltpu.VMEM((2, rows, half), BF16),
            pltpu.VMEM((2, rows, half), BF16),
            pltpu.VMEM((rows, feat), F32),
            pltpu.VMEM((rows, feat), F32),
            dma((8,)),
            dma((2 + reach,)),
            dma(()),
            dma((flows,)),
            dma((flows,)),
            dma((2,)),
            dma((2,)),
            dma((2 * SPAN,)),
            dma((2 * SPAN,)),
            dma((2 * SPAN,)),
            dma((2 * SPAN,)),
            dma((flows,)),
            dma((flows,)),
            dma((2,)),
            dma((2,)),
        ],
        compiler_params=pltpu.CompilerParams(
            collective_id=0, has_side_effects=True, vmem_limit_bytes=56 * 1024 * 1024
        ),
    )(
        dest_block,
        col_tile,
        tile_count,
        node_feats,
        edge_tiles,
        w_self,
        w_agg,
        in_bias[None],
        w_out,
        out_gain[None],
        grad_out,
    )


def solution(mesh):
    shards = ("blk", "grp")
    return jax.shard_map(
        body,
        mesh=mesh,
        in_specs=(
            P(shards, None),
            P(shards, None),
            P(shards, None),
            P(shards),
            P(shards, None, None, None),
            P(),
            P(),
            P(),
            P(),
            P(),
            P(shards, None),
        ),
        out_specs=(P(shards, None), P(shards, None), P(shards, None, None, None)),
        check_vma=False,
    )
```

time: 435 us -> 83.5 us (0.19); the launches traced: 430 us -> 83.2 us
  waiting for transfers between devices: 336 us -> 0 us
  Pallas kernels: 0 us -> 77.6 us
  starting transfers between devices: 45.2 us -> 0 us
  local copies, waits for them, and re-layouts: 19.4 us -> 4.35 us
  between operations: 15.1 us -> 1.3 us
  matrix products: 10.4 us -> 0 us
    reduce_scatter x1 -> x0, waiting for transfers between devices: 214 us -> none  [body(): lax.psum_scatter(rows_sum.reshape(lax.axis_size('grp') * row_count, feat_...]
    all_gather x1 -> x0, waiting for transfers between devices: 110 us -> none  [body(): gathered = lax.all_gather(feat_bf, 'grp', axis=0, tiled=True)]
    pallas_call x0 -> x1, Pallas kernels: none -> 77.6 us  [body(): pl.pallas_call(kernel, out_shape=(jax.ShapeDtypeStruct((rows, feat), F32)...]
    ppermute x12 -> x0, starting transfers between devices: 45.1 us -> none  [passed_along(): return lax.ppermute(value, axis, pairs)]
    ppermute x12 -> x0, waiting for transfers between devices: 12.5 us -> none  [passed_along(): return lax.ppermute(value, axis, pairs)]
    dot_general x11 -> x0, matrix products: 10.4 us -> none  [the longest x1 2.37 us: body(): jnp.dot(col_hot, flat_terms, precision=top_precision, preferred_element_t...]
  transfers between devices with their start and end apart: 14 -> 0, of which waited for: 5 -> 0; matrix products, arithmetic and copies ran while one was open for 2% -> 0% of each run, Pallas kernels for 0% -> 0%
where the time goes in v1:
time: 83.5 us; the launch traced here: 83.2 us
  Pallas kernels  77.6 us (93%)
  local copies, waits for them, and re-layouts  4.35 us (5%)
  between operations  1.3 us (2%)
    pallas_call x1, Pallas kernels, body(): pl.pallas_call(kernel, out_shape=(jax.ShapeDtypeStruct((rows, feat), F32)...  77.6 us
    unnamed x5, local copies, waits for them, and re-layouts  4.35 us

profile of v1, /device:TPU:1, one launch (start us, length us, event | category | flops | bytes accessed | tf_op | source)
XLA Modules:
  0.0 83.2 jit_solution(11452619936092529871)
XLA Ops:
  1.3 77.6 %shard_map.130 = (f32[128,256]{1,0:T(8,128)}, f32[128,256]{1,0:T(8,128)}, bf16[1,24,128,128]{3,2,1,0:T(8,128)(2,1)}) custom-call(s32[1,24]{1,0:T(1,128)} %dest_ref.1, s32[1,24]{1,0:T(1,128)} %col_ref.1, s32[1]{0:T(128)S(6)} %copy.17.count_ref, f32[128,256]{1,0:T(8,128)} %feats_hbm.1, bf16[1,24,128,128]{3,2,1,0:T(8,128)(2,1)} %edge_hbm.1, ...), custom_call_target="tpu_custom_call" | custom-call | tf_op jit(solution)/shard_map/pallas_call | solution.py:420
  78.9 0.0 copy-start
  78.9 1.6 %copy.18 = f32[128,256]{1,0:T(8,128)} copy(f32[128,256]{1,0:T(8,128)} %get-tuple-element.6) | data formatting | bytes 262144
  80.5 0.0 copy-done
  80.5 0.7 copy.19
  81.1 2.1 %copy.20 = bf16[1,24,128,128]{3,2,1,0:T(8,128)(2,1)} copy(bf16[1,24,128,128]{3,2,1,0:T(8,128)(2,1)} %get-tuple-element.8) | data formatting | bytes 1572864
Async XLA Ops:
  78.9 1.6 %copy-start = (f32[128,256]{1,0:T(8,128)S(1)}, f32[128,256]{1,0:T(8,128)}, u32[]{:S(2)}) copy-start(f32[128,256]{1,0:T(8,128)} %get-tuple-element.7) | copy-start | bytes 393220

commit v2 on v1

v2 whole, which is shorter than its diff:
```python
import jax
import jax.numpy as jnp
from jax import lax
from jax.experimental import pallas as pl
from jax.experimental.pallas import tpu as pltpu
from jax.sharding import PartitionSpec as P

HALO = 3
SPAN = 2 * HALO + 1
LN_EPS = 1e-05
BF16 = jnp.bfloat16
F32 = jnp.float32


def matmul(left, right):
    return jnp.dot(left, right, preferred_element_type=F32)


def matmul_nt(left, right):
    return lax.dot_general(left, right, (((1,), (1,)), ((), ())), preferred_element_type=F32)


def kernel(
    dest_hbm,
    col_hbm,
    count_hbm,
    feats_hbm,
    edge_hbm,
    w_self_hbm,
    w_agg_hbm,
    bias_hbm,
    w_out_hbm,
    gain_hbm,
    grad_hbm,
    updated_hbm,
    grad_x_hbm,
    tile_grads_hbm,
    dest,
    col,
    count,
    feats,
    edge,
    w_self,
    w_agg,
    bias,
    w_out,
    gain,
    grad,
    updated,
    grad_x,
    tile_grads,
    table_v,
    table,
    edge_t,
    dense,
    dense_t,
    gathered,
    part_out,
    part_in,
    near,
    red_out,
    red_in,
    swap_out,
    swap_in,
    messages,
    pre_base,
    own_grad,
    local_sems,
    out_sems,
    table_sem,
    ring_send,
    ring_recv,
    pair_send,
    pair_recv,
    part_send,
    part_recv,
    near_send,
    near_recv,
    red_send,
    red_recv,
    swap_send,
    swap_recv,
):
    rows = feats.shape[0]
    half = feats.shape[1] // 2
    slots = edge.shape[0] - 1
    members = gathered.shape[1]
    ring = members // 2
    reach = ring // 2
    blocks = lax.axis_size("blk")
    blk = lax.axis_index("blk")
    grp = lax.axis_index("grp")
    ring_at = grp // 2
    plane = grp % 2
    side = 2 * (blk % 2) - 1

    def member(ring_pos, q):
        return lax.rem(ring_pos + 2 * ring, ring) * 2 + (plane if q == 0 else 1 - plane)

    def to_ring(hop):
        return {"grp": member(ring_at + hop, 0)}

    def to_pair():
        return {"grp": member(ring_at, 1)}

    def to_blk(offset):
        return {"blk": lax.rem(blk + offset * side + blocks, blocks)}

    sent = []
    stores = []

    def send(copy):
        copy.start()
        sent.append(copy)

    def arrive(copy):
        copy.wait_recv()

    def finish():
        for copy in sent:
            copy.wait_send()
        for store in stores:
            store.wait()

    barrier = pltpu.get_barrier_semaphore()
    greeted = [to_pair()]
    greeted += [to_ring(hop) for hop in (-2, -1, 1, 2)]
    greeted += [to_blk(offset) for offset in (-1, 1, 2, -2, 3, -3)]
    for target in greeted:
        pl.semaphore_signal(barrier, inc=1, device_id=target, device_id_type=pl.DeviceIdType.MESH)

    loads = [
        pltpu.make_async_copy(src, dst, local_sems.at[i])
        for i, (src, dst) in enumerate(
            [
                (feats_hbm, feats),
                (dest_hbm, dest),
                (col_hbm, col),
                (count_hbm, count),
                (edge_hbm.at[0], edge.at[pl.ds(0, slots)]),
                (w_self_hbm, w_self),
                (bias_hbm, bias),
                (w_agg_hbm, w_agg),
                (w_out_hbm, w_out),
                (gain_hbm, gain),
                (grad_hbm, grad),
            ]
        )
    ]
    for load in loads:
        load.start()

    loads[0].wait()
    feat_bf = feats[...].astype(BF16)
    mine = member(ring_at, 0)
    for h in range(2):
        gathered[h, mine] = feat_bf[:, h * half : (h + 1) * half]

    pl.semaphore_wait(barrier, len(greeted))

    def ring_id(h, q, direction, d):
        return ((h * 2 + q) * 2 + direction) * reach + d - 1

    def in_flow(q, direction, d):
        return d < reach or direction == q and d == reach

    def ring_copy(h, q, direction, d, incoming=False):
        sign = 1 if direction == 0 else -1
        start = d - 1 if q == 0 else (0 if d <= 2 else 2)
        at = member(ring_at - sign * (d if incoming else start), q)
        i = ring_id(h, q, direction, d)
        return pltpu.make_async_remote_copy(
            src_ref=gathered.at[h, at],
            dst_ref=gathered.at[h, at],
            send_sem=ring_send.at[i],
            recv_sem=ring_recv.at[i],
            device_id=to_ring(sign * (d - start)),
            device_id_type=pl.DeviceIdType.MESH,
        )

    def pair_copy(h, incoming=False):
        at = member(ring_at, 1 if incoming else 0)
        return pltpu.make_async_remote_copy(
            src_ref=gathered.at[h, at],
            dst_ref=gathered.at[h, at],
            send_sem=pair_send.at[h],
            recv_sem=pair_recv.at[h],
            device_id=to_pair(),
            device_id_type=pl.DeviceIdType.MESH,
        )

    def ring_sends(h, q, *distances):
        for d in distances:
            for direction in range(2):
                if in_flow(q, direction, d):
                    send(ring_copy(h, q, direction, d))

    def ring_arrives(h, q, *distances):
        for d in distances:
            for direction in range(2):
                if in_flow(q, direction, d):
                    arrive(ring_copy(h, q, direction, d, incoming=True))

    def ring_arrives_last(h):
        ring_arrives(h, 1, 1, 3, 4)
        ring_arrives(h, 0, reach)

    for h in range(2):
        send(pair_copy(h))
        ring_sends(h, 0, 1)

    for load in loads[1:4]:
        load.wait()
    lane = lax.broadcasted_iota(jnp.int32, table_v.shape, 1)
    found = jnp.full(table_v.shape, slots, jnp.int32)
    for t in range(slots):
        rel = lax.rem(dest[0, t] - blk + HALO + blocks, blocks)
        key = jnp.where(t < count[0], rel * members + col[0, t], -1)
        found = jnp.where(lane == key, t, found)
    table_v[...] = found
    table_copy = pltpu.make_async_copy(table_v, table, table_sem)
    table_copy.start()

    loads[4].wait()
    edge[slots] = jnp.zeros((rows, rows), BF16)
    edge_t[slots] = jnp.zeros((rows, rows), BF16)

    def turn(t, carry):
        edge_t[t] = edge[t].T
        return carry

    def fill_dense(n, carry):
        for c in range(members):
            dense[n, :, c * rows : (c + 1) * rows] = edge[table[0, n * members + c]]
        return carry

    def fill_dense_t(q):
        def fill(k, carry):
            at = member(ring_at + k, q)
            for n in range(SPAN):
                dense_t[q, k, :, n * rows : (n + 1) * rows] = edge_t[table[0, n * members + at]]
            return carry

        lax.fori_loop(0, ring, fill, 0)

    for h in range(2):
        ring_arrives(h, 0, 1)
        ring_sends(h, 0, 2)
    table_copy.wait()
    lax.fori_loop(0, 3, fill_dense, 0)
    for h in range(2):
        ring_arrives(h, 0, 2)
        ring_sends(h, 0, 3)
    lax.fori_loop(3, SPAN, fill_dense, 0)
    for h in range(2):
        arrive(pair_copy(h, incoming=True))
        ring_sends(h, 1, 1, 2)
    for h in range(2):
        ring_arrives(h, 0, 3)
        ring_sends(h, 0, 4)
    lax.fori_loop(0, slots, turn, 0, unroll=2)
    for h in range(2):
        ring_arrives(h, 1, 2)
        ring_sends(h, 1, 3, 4)

    def part_copy(h, offset):
        i = h * SPAN + HALO + offset
        return pltpu.make_async_remote_copy(
            src_ref=part_out.at[h, HALO + offset],
            dst_ref=part_in.at[h, HALO + offset],
            send_sem=part_send.at[i],
            recv_sem=part_recv.at[i],
            device_id=to_blk(offset),
            device_id_type=pl.DeviceIdType.MESH,
        )

    centre = []
    for h in range(2):
        ring_arrives_last(h)
        columns = gathered[h].reshape(members * rows, half)
        for offset in (3, -3, 2, -2, 1, -1):
            partial = matmul(dense[HALO + offset * side], columns)
            part_out[h, HALO + offset] = partial.astype(BF16)
            send(part_copy(h, offset))
        centre.append(matmul(dense[HALO], columns))

    loads[5].wait()
    loads[6].wait()
    pre_base[...] = matmul(feat_bf, w_self[...]) + bias[...]
    for q in (1, 0):
        fill_dense_t(q)
    for load in loads[7:]:
        load.wait()

    pre_act = pre_base[...]
    for h in range(2):
        total = centre[h]
        for offset in (-1, 1, -2, 2, -3, 3):
            arrive(part_copy(h, offset))
            total = total + part_in[h, HALO + offset].astype(F32)
        pre_act = pre_act + matmul(total.astype(BF16), w_agg[h * half : (h + 1) * half, :])
    sigmoid_z = jax.nn.sigmoid(pre_act)
    hidden = (pre_act * sigmoid_z).astype(BF16)
    mixed = matmul(hidden, w_out[...])
    centred = mixed - jnp.mean(mixed, axis=-1, keepdims=True)
    variance = jnp.mean(centred * centred, axis=-1, keepdims=True)
    inv_std = lax.rsqrt(variance + LN_EPS)
    normed = centred * inv_std

    g_norm = grad[...] * gain[...]
    g_mixed = inv_std * (
        g_norm
        - jnp.mean(g_norm, axis=-1, keepdims=True)
        - normed * jnp.mean(g_norm * normed, axis=-1, keepdims=True)
    )
    g_hidden = matmul_nt(g_mixed.astype(BF16), w_out[...])
    g_pre = (g_hidden * sigmoid_z * (1.0 + pre_act * (1.0 - sigmoid_z))).astype(BF16)

    def near_copy(h, kind, incoming=False):
        source = 0 if kind < 4 else kind - 3
        target = {0: -1, 1: 1, 2: -2, 3: 3, 4: -1, 5: -1}[kind]
        lands = {0: -1, 1: 1, 2: 2, 3: 3, 4: -2, 5: -3}[kind] if incoming else source - target
        i = h * 6 + kind
        return pltpu.make_async_remote_copy(
            src_ref=near.at[h, HALO + source * side],
            dst_ref=near.at[h, HALO + lands * side],
            send_sem=near_send.at[i],
            recv_sem=near_recv.at[i],
            device_id=to_blk(target),
            device_id_type=pl.DeviceIdType.MESH,
        )

    for h in range(2):
        near[h, HALO] = matmul_nt(g_pre, w_agg[h * half : (h + 1) * half, :]).astype(BF16)
        for kind in (2, 1, 3, 0):
            send(near_copy(h, kind))

    updated[...] = feats[...] + gain[...] * normed
    stores.append(pltpu.make_async_copy(updated, updated_hbm, out_sems.at[0]))
    stores[-1].start()
    own_grad[...] = grad[...] + matmul_nt(g_pre, w_self[...])

    def red_flow(q, direction, d):
        return d < reach or direction == q and d == reach

    def red_hop(q, d):
        return 1 if q == 0 else (1 if d % 2 else 2)

    def red_copy(h, q, direction, d):
        i = ring_id(h, q, direction, d)
        return pltpu.make_async_remote_copy(
            src_ref=red_out.at[i],
            dst_ref=red_in.at[i],
            send_sem=red_send.at[i],
            recv_sem=red_recv.at[i],
            device_id=to_ring((1 if direction == 0 else -1) * red_hop(q, d)),
            device_id_type=pl.DeviceIdType.MESH,
        )

    def make_messages(h, q):
        made = matmul(
            dense_t[q].reshape(ring * rows, SPAN * rows), near[h].reshape(SPAN * rows, half)
        )
        messages[h, q] = made.reshape(ring, rows, half)

    def add_arrived(total, h, q, direction, distances):
        for d in distances:
            if red_flow(q, direction, d):
                arrive(red_copy(h, q, direction, d))
                total = total + red_in[ring_id(h, q, direction, d)].astype(F32)
        return total

    def red_sends(h, q, *distances):
        for d in distances:
            for direction in range(2):
                if red_flow(q, direction, d):
                    total = messages[h, q, (d if direction == 0 else -d) % ring]
                    earlier = [d + 1] if q == 0 else ([3, 4] if d == 2 else [])
                    total = add_arrived(total, h, q, direction, earlier)
                    red_out[ring_id(h, q, direction, d)] = total.astype(BF16)
                    send(red_copy(h, q, direction, d))

    def red_total(h, q):
        total = messages[h, q, 0]
        for direction in range(2):
            total = add_arrived(total, h, q, direction, [1, 2] if q else [1])
        return total

    def swap_copy(h):
        return pltpu.make_async_remote_copy(
            src_ref=swap_out.at[h],
            dst_ref=swap_in.at[h],
            send_sem=swap_send.at[h],
            recv_sem=swap_recv.at[h],
            device_id=to_pair(),
            device_id_type=pl.DeviceIdType.MESH,
        )

    def swap_sends(h):
        swap_out[h] = red_total(h, 1).astype(BF16)
        send(swap_copy(h))

    def tile_gradient(t, carry):
        rel = jnp.clip(lax.rem(dest[0, t] - blk + HALO + blocks, blocks), 0, SPAN - 1)
        at = jnp.clip(col[0, t], 0, members - 1)
        left = jnp.concatenate([near[0, rel], near[1, rel]], axis=1)
        right = jnp.concatenate([gathered[0, at], gathered[1, at]], axis=1)
        value = matmul_nt(left, right)
        tile_grads[t] = jnp.where(t < count[0], value, 0.0).astype(BF16)
        return carry

    share = slots // 4

    def tile_share(k):
        lax.fori_loop(k * share, (k + 1) * share, tile_gradient, 0, unroll=3 if share % 3 == 0 else 1)
        store = pltpu.make_async_copy(
            tile_grads.at[pl.ds(k * share, share)],
            tile_grads_hbm.at[0, pl.ds(k * share, share)],
            out_sems.at[2 + k],
        )
        store.start()
        stores.append(store)

    for h in range(2):
        for kind in (1, 2):
            arrive(near_copy(h, kind, incoming=True))
            send(near_copy(h, kind + 3))
        for kind in (0, 3, 4, 5):
            arrive(near_copy(h, kind, incoming=True))
        make_messages(h, 1)
        red_sends(h, 1, 4, 3)
        make_messages(h, 0)
        red_sends(h, 0, 4)
        red_sends(h, 1, 1)
    for h in range(2):
        red_sends(h, 1, 2)
        red_sends(h, 0, 3)
    tile_share(0)
    tile_share(1)
    for h in range(2):
        swap_sends(h)
    for h in range(2):
        red_sends(h, 0, 2)
    tile_share(2)
    for h in range(2):
        red_sends(h, 0, 1)
    tile_share(3)
    for h in range(2):
        total = red_total(h, 0)
        arrive(swap_copy(h))
        total = total + swap_in[h].astype(F32)
        at = slice(h * half, (h + 1) * half)
        grad_x[:, at] = own_grad[:, at] + total
    stores.append(pltpu.make_async_copy(grad_x, grad_x_hbm, out_sems.at[1]))
    stores[-1].start()

    finish()


def deliver(*refs):
    sources, targets, held = refs[:3], refs[3:6], refs[6:9]
    load_sems, store_sems = refs[9:]
    count = sources[2].shape[1] // 4
    pieces = [(2, (0, pl.ds(k * count, count))) for k in range(4)] + [(0, ...), (1, ...)]
    loads = [
        pltpu.make_async_copy(sources[a].at[at], held[a].at[at], load_sems.at[i])
        for i, (a, at) in enumerate(pieces)
    ]
    stores = [
        pltpu.make_async_copy(held[a].at[at], targets[a].at[at], store_sems.at[i])
        for i, (a, at) in enumerate(pieces)
    ]
    for load in loads:
        load.start()
    for load, store in zip(loads, stores):
        load.wait()
        store.start()
    for store in stores:
        store.wait()


def body(
    node_feats,
    dest_block,
    col_tile,
    tile_count,
    edge_tiles,
    w_self,
    w_agg,
    in_bias,
    w_out,
    out_gain,
    grad_out,
):
    rows, feat = node_feats.shape
    half = feat // 2
    slots = dest_block.shape[1]
    members = lax.axis_size("grp")
    reach = members // 4
    flows = 8 * reach
    table_lanes = -(-SPAN * members // 128) * 128
    anywhere = pl.BlockSpec(memory_space=pl.ANY)
    dma = pltpu.SemaphoreType.DMA
    results = (
        jax.ShapeDtypeStruct((rows, feat), F32),
        jax.ShapeDtypeStruct((rows, feat), F32),
        jax.ShapeDtypeStruct((1, slots, rows, rows), BF16),
    )
    made = pl.pallas_call(
        kernel,
        out_shape=results,
        in_specs=[anywhere] * 11,
        out_specs=[anywhere] * 3,
        scratch_shapes=[
            pltpu.SMEM((1, slots), jnp.int32),
            pltpu.SMEM((1, slots), jnp.int32),
            pltpu.SMEM((1,), jnp.int32),
            pltpu.VMEM((rows, feat), F32),
            pltpu.VMEM((slots + 1, rows, rows), BF16),
            pltpu.VMEM((feat, feat), BF16),
            pltpu.VMEM((feat, feat), BF16),
            pltpu.VMEM((1, feat), F32),
            pltpu.VMEM((feat, feat), BF16),
            pltpu.VMEM((1, feat), F32),
            pltpu.VMEM((rows, feat), F32),
            pltpu.VMEM((rows, feat), F32),
            pltpu.VMEM((rows, feat), F32),
            pltpu.VMEM((slots, rows, rows), BF16),
            pltpu.VMEM((1, table_lanes), jnp.int32),
            pltpu.SMEM((1, table_lanes), jnp.int32),
            pltpu.VMEM((slots + 1, rows, rows), BF16),
            pltpu.VMEM((SPAN, rows, members * rows), BF16),
            pltpu.VMEM((2, members // 2, rows, SPAN * rows), BF16),
            pltpu.VMEM((2, members, rows, half), BF16),
            pltpu.VMEM((2, SPAN, rows, half), BF16),
            pltpu.VMEM((2, SPAN, rows, half), BF16),
            pltpu.VMEM((2, SPAN, rows, half), BF16),
            pltpu.VMEM((flows, rows, half), BF16),
            pltpu.VMEM((flows, rows, half), BF16),
            pltpu.VMEM((4, rows, half), BF16),
            pltpu.VMEM((4, rows, half), BF16),
            pltpu.VMEM((2, 2, members // 2, rows, half), F32),
            pltpu.VMEM((rows, feat), F32),
            pltpu.VMEM((rows, feat), F32),
            dma((11,)),
            dma((6,)),
            dma(()),
            dma((flows,)),
            dma((flows,)),
            dma((4,)),
            dma((4,)),
            dma((2 * SPAN,)),
            dma((2 * SPAN,)),
            dma((12,)),
            dma((12,)),
            dma((flows,)),
            dma((flows,)),
            dma((4,)),
            dma((4,)),
        ],
        compiler_params=pltpu.CompilerParams(
            collective_id=0, has_side_effects=True, vmem_limit_bytes=56 * 1024 * 1024
        ),
    )(
        dest_block,
        col_tile,
        tile_count,
        node_feats,
        edge_tiles,
        w_self,
        w_agg,
        in_bias[None],
        w_out,
        out_gain[None],
        grad_out,
    )
    return pl.pallas_call(
        deliver,
        out_shape=results,
        in_specs=[anywhere] * 3,
        out_specs=[anywhere] * 3,
        scratch_shapes=[pltpu.VMEM(made_one.shape, made_one.dtype) for made_one in results]
        + [dma((6,)), dma((6,))],
        compiler_params=pltpu.CompilerParams(vmem_limit_bytes=56 * 1024 * 1024),
    )(*made)


def solution(mesh):
    shards = ("blk", "grp")
    return jax.shard_map(
        body,
        mesh=mesh,
        in_specs=(
            P(shards, None),
            P(shards, None),
            P(shards, None),
            P(shards),
            P(shards, None, None, None),
            P(),
            P(),
            P(),
            P(),
            P(),
            P(shards, None),
        ),
        out_specs=(P(shards, None), P(shards, None), P(shards, None, None, None)),
        check_vma=False,
    )
```

time: 83.5 us -> 78.7 us (0.943); the launches traced: 83.2 us -> 77.2 us
  local copies, waits for them, and re-layouts: 4.35 us -> 0 us
  Pallas kernels: 77.6 us -> 75.9 us
    unnamed x5 -> x0, local copies, waits for them, and re-layouts: 4.35 us -> none
    pallas_call x1 -> x2, Pallas kernels: 77.6 us -> 75.9 us  [the longest x1 73.8 us: body(): pl.pallas_call(kernel, out_shape=results, in_specs=[anywhere] * 11, out_s...]
where the time goes in v2:
time: 78.7 us; the launch traced here: 77.2 us
  Pallas kernels  75.9 us (96%)
  between operations  1.29 us (2%)
    pallas_call x1, Pallas kernels, body(): pl.pallas_call(kernel, out_shape=results, in_specs=[anywhere] * 11, out_s...  73.8 us
    pallas_call x1, Pallas kernels, body(): pl.pallas_call(deliver, out_shape=results, in_specs=[anywhere] * 3, out_s...  2.09 us

profile of v2, /device:TPU:1, one launch (start us, length us, event | category | flops | bytes accessed | tf_op | source)
XLA Modules:
  0.0 77.2 jit_solution(6334966674150430402)
XLA Ops:
  1.3 73.8 %shard_map.130 = (f32[128,256]{1,0:T(8,128)}, f32[128,256]{1,0:T(8,128)}, bf16[1,24,128,128]{3,2,1,0:T(8,128)(2,1)}) custom-call(s32[1,24]{1,0:T(1,128)} %dest_hbm.1, s32[1,24]{1,0:T(1,128)} %col_hbm.1, s32[1]{0:T(128)S(6)} %copy.14.count_hbm, f32[128,256]{1,0:T(8,128)} %feats_hbm.1, bf16[1,24,128,128]{3,2,1,0:T(8,128)(2,1)} %edge_hbm.1, ...), custom_call_target="tpu_custom_call" | custom-call | tf_op jit(solution)/shard_map/pallas_call | solution.py:509
  75.1 2.1 %shard_map.131 = (f32[128,256]{1,0:T(8,128)}, f32[128,256]{1,0:T(8,128)}, bf16[1,24,128,128]{3,2,1,0:T(8,128)(2,1)}) custom-call(f32[128,256]{1,0:T(8,128)} %get-tuple-element.6.refs_0_, f32[128,256]{1,0:T(8,128)} %get-tuple-element.7.refs_1_, bf16[1,24,128,128]{3,2,1,0:T(8,128)(2,1)} %get-tuple-element.8.refs_2_), custom_call_target="tpu_custom_call" | custom-call | tf_op jit(solution)/shard_map/pallas_call | solution.py:577

commit v3 on v2

--- a/solution.py
+++ b/solution.py
@@ -32,9 +32,9 @@
     w_out_hbm,
     gain_hbm,
     grad_hbm,
-    updated_hbm,
-    grad_x_hbm,
-    tile_grads_hbm,
+    updated,
+    grad_x,
+    tile_grads,
     dest,
     col,
     count,
@@ -46,9 +46,6 @@
     w_out,
     gain,
     grad,
-    updated,
-    grad_x,
-    tile_grads,
     table_v,
     table,
     edge_t,
@@ -63,10 +60,11 @@
     swap_out,
     swap_in,
     messages,
+    w_agg_t,
+    w_out_t,
     pre_base,
     own_grad,
     local_sems,
-    out_sems,
     table_sem,
     ring_send,
     ring_recv,
@@ -107,7 +105,6 @@
         return {"blk": lax.rem(blk + offset * side + blocks, blocks)}
 
     sent = []
-    stores = []
 
     def send(copy):
         copy.start()
@@ -119,8 +116,6 @@
     def finish():
         for copy in sent:
             copy.wait_send()
-        for store in stores:
-            store.wait()
 
     barrier = pltpu.get_barrier_semaphore()
     greeted = [to_pair()]
@@ -254,14 +249,16 @@
     lax.fori_loop(3, SPAN, fill_dense, 0)
     for h in range(2):
         arrive(pair_copy(h, incoming=True))
-        ring_sends(h, 1, 1, 2)
+        ring_sends(h, 1, 2)
+    for h in range(2):
+        ring_sends(h, 1, 1)
     for h in range(2):
         ring_arrives(h, 0, 3)
         ring_sends(h, 0, 4)
     lax.fori_loop(0, slots, turn, 0, unroll=2)
     for h in range(2):
         ring_arrives(h, 1, 2)
-        ring_sends(h, 1, 3, 4)
+        ring_sends(h, 1, 4, 3)
 
     def part_copy(h, offset):
         i = h * SPAN + HALO + offset
@@ -291,6 +288,8 @@
         fill_dense_t(q)
     for load in loads[7:]:
         load.wait()
+    w_agg_t[...] = w_agg[...].T
+    w_out_t[...] = w_out[...].T
 
     pre_act = pre_base[...]
     for h in range(2):
@@ -313,7 +312,7 @@
         - jnp.mean(g_norm, axis=-1, keepdims=True)
         - normed * jnp.mean(g_norm * normed, axis=-1, keepdims=True)
     )
-    g_hidden = matmul_nt(g_mixed.astype(BF16), w_out[...])
+    g_hidden = matmul(g_mixed.astype(BF16), w_out_t[...])
     g_pre = (g_hidden * sigmoid_z * (1.0 + pre_act * (1.0 - sigmoid_z))).astype(BF16)
 
     def near_copy(h, kind, incoming=False):
@@ -331,13 +330,11 @@
         )
 
     for h in range(2):
-        near[h, HALO] = matmul_nt(g_pre, w_agg[h * half : (h + 1) * half, :]).astype(BF16)
+        near[h, HALO] = matmul(g_pre, w_agg_t[:, h * half : (h + 1) * half]).astype(BF16)
         for kind in (2, 1, 3, 0):
             send(near_copy(h, kind))
 
     updated[...] = feats[...] + gain[...] * normed
-    stores.append(pltpu.make_async_copy(updated, updated_hbm, out_sems.at[0]))
-    stores[-1].start()
     own_grad[...] = grad[...] + matmul_nt(g_pre, w_self[...])
 
     def red_flow(q, direction, d):
@@ -406,20 +403,13 @@
         left = jnp.concatenate([near[0, rel], near[1, rel]], axis=1)
         right = jnp.concatenate([gathered[0, at], gathered[1, at]], axis=1)
         value = matmul_nt(left, right)
-        tile_grads[t] = jnp.where(t < count[0], value, 0.0).astype(BF16)
+        tile_grads[0, t] = jnp.where(t < count[0], value, 0.0).astype(BF16)
         return carry
 
     share = slots // 4
 
     def tile_share(k):
         lax.fori_loop(k * share, (k + 1) * share, tile_gradient, 0, unroll=3 if share % 3 == 0 else 1)
-        store = pltpu.make_async_copy(
-            tile_grads.at[pl.ds(k * share, share)],
-            tile_grads_hbm.at[0, pl.ds(k * share, share)],
-            out_sems.at[2 + k],
-        )
-        store.start()
-        stores.append(store)
 
     for h in range(2):
         for kind in (1, 2):
@@ -436,14 +426,13 @@
         red_sends(h, 1, 2)
         red_sends(h, 0, 3)
     tile_share(0)
+    for h in range(2):
+        swap_sends(h)
+        red_sends(h, 0, 2)
     tile_share(1)
     for h in range(2):
-        swap_sends(h)
-    for h in range(2):
-        red_sends(h, 0, 2)
+        red_sends(h, 0, 1)
     tile_share(2)
-    for h in range(2):
-        red_sends(h, 0, 1)
     tile_share(3)
     for h in range(2):
         total = red_total(h, 0)
@@ -451,32 +440,22 @@
         total = total + swap_in[h].astype(F32)
         at = slice(h * half, (h + 1) * half)
         grad_x[:, at] = own_grad[:, at] + total
-    stores.append(pltpu.make_async_copy(grad_x, grad_x_hbm, out_sems.at[1]))
-    stores[-1].start()
 
     finish()
 
 
 def deliver(*refs):
-    sources, targets, held = refs[:3], refs[3:6], refs[6:9]
-    load_sems, store_sems = refs[9:]
+    sources, targets, sems = refs[:3], refs[3:6], refs[6]
     count = sources[2].shape[1] // 4
     pieces = [(2, (0, pl.ds(k * count, count))) for k in range(4)] + [(0, ...), (1, ...)]
-    loads = [
-        pltpu.make_async_copy(sources[a].at[at], held[a].at[at], load_sems.at[i])
+    copies = [
+        pltpu.make_async_copy(sources[a].at[at], targets[a].at[at], sems.at[i])
         for i, (a, at) in enumerate(pieces)
     ]
-    stores = [
-        pltpu.make_async_copy(held[a].at[at], targets[a].at[at], store_sems.at[i])
-        for i, (a, at) in enumerate(pieces)
-    ]
-    for load in loads:
-        load.start()
-    for load, store in zip(loads, stores):
-        load.wait()
-        store.start()
-    for store in stores:
-        store.wait()
+    for copy in copies:
+        copy.start()
+    for copy in copies:
+        copy.wait()
 
 
 def body(
@@ -500,6 +479,7 @@
     flows = 8 * reach
     table_lanes = -(-SPAN * members // 128) * 128
     anywhere = pl.BlockSpec(memory_space=pl.ANY)
+    in_vmem = pl.BlockSpec(memory_space=pltpu.VMEM)
     dma = pltpu.SemaphoreType.DMA
     results = (
         jax.ShapeDtypeStruct((rows, feat), F32),
@@ -508,9 +488,9 @@
     )
     made = pl.pallas_call(
         kernel,
-        out_shape=results,
+        out_shape=tuple(pltpu.VMEM(r.shape, r.dtype) for r in results),
         in_specs=[anywhere] * 11,
-        out_specs=[anywhere] * 3,
+        out_specs=[in_vmem] * 3,
         scratch_shapes=[
             pltpu.SMEM((1, slots), jnp.int32),
             pltpu.SMEM((1, slots), jnp.int32),
@@ -523,9 +503,6 @@
             pltpu.VMEM((feat, feat), BF16),
             pltpu.VMEM((1, feat), F32),
             pltpu.VMEM((rows, feat), F32),
-            pltpu.VMEM((rows, feat), F32),
-            pltpu.VMEM((rows, feat), F32),
-            pltpu.VMEM((slots, rows, rows), BF16),
             pltpu.VMEM((1, table_lanes), jnp.int32),
             pltpu.SMEM((1, table_lanes), jnp.int32),
             pltpu.VMEM((slots + 1, rows, rows), BF16),
@@ -540,10 +517,11 @@
             pltpu.VMEM((4, rows, half), BF16),
             pltpu.VMEM((4, rows, half), BF16),
             pltpu.VMEM((2, 2, members // 2, rows, half), F32),
+            pltpu.VMEM((feat, feat), BF16),
+            pltpu.VMEM((feat, feat), BF16),
             pltpu.VMEM((rows, feat), F32),
             pltpu.VMEM((rows, feat), F32),
             dma((11,)),
-            dma((6,)),
             dma(()),
             dma((flows,)),
             dma((flows,)),
@@ -577,12 +555,11 @@
     return pl.pallas_call(
         deliver,
         out_shape=results,
-        in_specs=[anywhere] * 3,
+        in_specs=[in_vmem] * 3,
         out_specs=[anywhere] * 3,
-        scratch_shapes=[pltpu.VMEM(made_one.shape, made_one.dtype) for made_one in results]
-        + [dma((6,)), dma((6,))],
+        scratch_shapes=[dma((6,))],
         compiler_params=pltpu.CompilerParams(vmem_limit_bytes=56 * 1024 * 1024),
-    )(*made)
+    )(*[pltpu.with_memory_space_constraint(one, pltpu.VMEM) for one in made])
 
 
 def solution(mesh):

time: 78.7 us -> 76.2 us (0.968)
  the two profiles are of different devices: /device:TPU:1 before, /device:TPU:16 now
where the time goes in v3:
time: 76.2 us; the launch traced here: 76 us
  Pallas kernels  74.8 us (98%)
  between operations  1.29 us (2%)
    pallas_call x1, Pallas kernels, body(): pl.pallas_call(kernel, out_shape=tuple((pltpu.VMEM(r.shape, r.dtype) for...  73.7 us

profile of v3, /device:TPU:16, one launch (start us, length us, event | category | flops | bytes accessed | tf_op | source)
XLA Modules:
  0.0 76.0 jit_solution(15813072559460685737)
XLA Ops:
  1.3 73.7 %shard_map.130 = (f32[128,256]{1,0:T(8,128)S(1)}, f32[128,256]{1,0:T(8,128)S(1)}, bf16[1,24,128,128]{3,2,1,0:T(8,128)(2,1)S(1)}) custom-call(s32[1,24]{1,0:T(1,128)} %dest_hbm.1, s32[1,24]{1,0:T(1,128)} %col_hbm.1, s32[1]{0:T(128)S(6)} %copy.14.count_hbm, f32[128,256]{1,0:T(8,128)} %feats_hbm.1, bf16[1,24,128,128]{3,2,1,0:T(8,128)(2,1)} %edge_hbm.1, ...), custom_call_target="tpu_custom_call" | custom-call | tf_op jit(solution)/shard_map/pallas_call | solution.py:489
  75.0 1.0 %shard_map.131 = (f32[128,256]{1,0:T(8,128)}, f32[128,256]{1,0:T(8,128)}, bf16[1,24,128,128]{3,2,1,0:T(8,128)(2,1)}) custom-call(f32[128,256]{1,0:T(8,128)S(1)} %get-tuple-element.6.refs_0_, f32[128,256]{1,0:T(8,128)S(1)} %get-tuple-element.7.refs_1_, bf16[1,24,128,128]{3,2,1,0:T(8,128)(2,1)S(1)} %get-tuple-element.8.refs_2_), custom_call_target="tpu_custom_call" | custom-call | tf_op jit(solution)/shard_map/pallas_call | solution.py:555

commit v4 on v3

--- a/solution.py
+++ b/solution.py
@@ -70,6 +70,7 @@
     ring_recv,
     pair_send,
     pair_recv,
+    pair_here,
     part_send,
     part_recv,
     near_send,
@@ -106,23 +107,30 @@
 
     sent = []
 
-    def send(copy):
-        copy.start()
-        sent.append(copy)
+    def send(copy, *which):
+        copy(*which).start()
+        sent.append((copy, which))
 
     def arrive(copy):
         copy.wait_recv()
 
     def finish():
-        for copy in sent:
-            copy.wait_send()
+        for copy, which in sent:
+            copy(*which).wait_send()
 
     barrier = pltpu.get_barrier_semaphore()
-    greeted = [to_pair()]
-    greeted += [to_ring(hop) for hop in (-2, -1, 1, 2)]
+    greeted = [to_ring(hop) for hop in (-2, -1, 1, 2)]
     greeted += [to_blk(offset) for offset in (-1, 1, 2, -2, 3, -3)]
+
+    def greet(semaphore, target):
+        pl.semaphore_signal(semaphore, inc=1, device_id=target, device_id_type=pl.DeviceIdType.MESH)
+
+    @pl.when(plane == 0)
+    def _():
+        greet(barrier, to_pair())
+
     for target in greeted:
-        pl.semaphore_signal(barrier, inc=1, device_id=target, device_id_type=pl.DeviceIdType.MESH)
+        greet(barrier, target)
 
     loads = [
         pltpu.make_async_copy(src, dst, local_sems.at[i])
@@ -151,35 +159,47 @@
     for h in range(2):
         gathered[h, mine] = feat_bf[:, h * half : (h + 1) * half]
 
-    pl.semaphore_wait(barrier, len(greeted))
+    pl.semaphore_wait(barrier, len(greeted) + plane)
+
+    @pl.when(plane == 1)
+    def _():
+        greet(pair_here, to_pair())
 
     def ring_id(h, q, direction, d):
-        return ((h * 2 + q) * 2 + direction) * reach + d - 1
-
-    def in_flow(q, direction, d):
-        return d < reach or direction == q and d == reach
+        return ((h * 2 + min(q, 1)) * 2 + direction) * reach + d - 1
+
+    def in_flow(h, q, direction, d):
+        if q == 2:
+            return d <= 3
+        return d < reach or direction == (q + h) % 2 and d == reach
 
     def ring_copy(h, q, direction, d, incoming=False):
         sign = 1 if direction == 0 else -1
-        start = d - 1 if q == 0 else (0 if d <= 2 else 2)
-        at = member(ring_at - sign * (d if incoming else start), q)
+        if q == 2:
+            hop = 1 if d == 3 else d
+            start = reach if d == 3 else 0
+            at = member(ring_at + start - (sign * hop if incoming else 0), 1)
+        else:
+            start = d - 1 if q == 0 else (0 if d <= 2 else 2)
+            hop = d - start
+            at = member(ring_at - sign * (d if incoming else start), q)
         i = ring_id(h, q, direction, d)
         return pltpu.make_async_remote_copy(
             src_ref=gathered.at[h, at],
             dst_ref=gathered.at[h, at],
             send_sem=ring_send.at[i],
             recv_sem=ring_recv.at[i],
-            device_id=to_ring(sign * (d - start)),
+            device_id=to_ring(sign * hop),
             device_id_type=pl.DeviceIdType.MESH,
         )
 
-    def pair_copy(h, incoming=False):
-        at = member(ring_at, 1 if incoming else 0)
+    def pair_copy(h, far=0, incoming=False):
+        at = member(ring_at + far * reach, 1 if incoming else 0)
         return pltpu.make_async_remote_copy(
             src_ref=gathered.at[h, at],
             dst_ref=gathered.at[h, at],
-            send_sem=pair_send.at[h],
-            recv_sem=pair_recv.at[h],
+            send_sem=pair_send.at[2 * far + h],
+            recv_sem=pair_recv.at[2 * far + h],
             device_id=to_pair(),
             device_id_type=pl.DeviceIdType.MESH,
         )
@@ -187,21 +207,47 @@
     def ring_sends(h, q, *distances):
         for d in distances:
             for direction in range(2):
-                if in_flow(q, direction, d):
-                    send(ring_copy(h, q, direction, d))
+                if in_flow(h, q, direction, d):
+                    if q == 0:
+                        send(ring_copy, h, q, direction, d)
+                    else:
+                        ring_copy(h, q, direction, d).start()
 
     def ring_arrives(h, q, *distances):
         for d in distances:
             for direction in range(2):
-                if in_flow(q, direction, d):
+                if in_flow(h, q, direction, d):
                     arrive(ring_copy(h, q, direction, d, incoming=True))
 
     def ring_arrives_last(h):
-        ring_arrives(h, 1, 1, 3, 4)
-        ring_arrives(h, 0, reach)
-
-    for h in range(2):
-        send(pair_copy(h))
+        @pl.when(plane == 0)
+        def _():
+            ring_arrives(h, 1, 1, 3, 4)
+
+        @pl.when(plane == 1)
+        def _():
+            ring_arrives(h, 2, 1, 3, 2)
+            ring_arrives(h, 0, 4)
+
+    def ring_leaves():
+        for q in (1, 2):
+
+            @pl.when(plane == q - 1)
+            def _(q=q):
+                for h in range(2):
+                    for direction in range(2):
+                        for d in range(1, reach + 1):
+                            if in_flow(h, q, direction, d):
+                                ring_copy(h, q, direction, d).wait_send()
+                    if q == 1:
+                        pair_copy(h, 1).wait_send()
+
+    @pl.when(plane == 1)
+    def _():
+        for h in range(2):
+            pair_copy(h).start()
+
+    for h in range(2):
         ring_sends(h, 0, 1)
 
     for load in loads[1:4]:
@@ -248,17 +294,37 @@
         ring_sends(h, 0, 3)
     lax.fori_loop(3, SPAN, fill_dense, 0)
     for h in range(2):
-        arrive(pair_copy(h, incoming=True))
-        ring_sends(h, 1, 2)
-    for h in range(2):
-        ring_sends(h, 1, 1)
-    for h in range(2):
         ring_arrives(h, 0, 3)
         ring_sends(h, 0, 4)
+
+    @pl.when(plane == 0)
+    def _():
+        pl.semaphore_wait(pair_here, 1)
+        for h in range(2):
+            pair_copy(h).start()
+            ring_arrives(h, 0, 4)
+            pair_copy(h, 1).start()
+        for h in range(2):
+            arrive(pair_copy(h, incoming=True))
+            ring_sends(h, 1, 2)
+        for h in range(2):
+            ring_sends(h, 1, 1)
+
     lax.fori_loop(0, slots, turn, 0, unroll=2)
-    for h in range(2):
-        ring_arrives(h, 1, 2)
-        ring_sends(h, 1, 4, 3)
+
+    @pl.when(plane == 0)
+    def _():
+        for h in range(2):
+            ring_arrives(h, 1, 2)
+            ring_sends(h, 1, 4, 3)
+
+    @pl.when(plane == 1)
+    def _():
+        for h in range(2):
+            arrive(pair_copy(h, incoming=True))
+            ring_sends(h, 2, 2, 1)
+            arrive(pair_copy(h, 1, incoming=True))
+            ring_sends(h, 2, 3)
 
     def part_copy(h, offset):
         i = h * SPAN + HALO + offset
@@ -278,7 +344,7 @@
         for offset in (3, -3, 2, -2, 1, -1):
             partial = matmul(dense[HALO + offset * side], columns)
             part_out[h, HALO + offset] = partial.astype(BF16)
-            send(part_copy(h, offset))
+            send(part_copy, h, offset)
         centre.append(matmul(dense[HALO], columns))
 
     loads[5].wait()
@@ -332,13 +398,10 @@
     for h in range(2):
         near[h, HALO] = matmul(g_pre, w_agg_t[:, h * half : (h + 1) * half]).astype(BF16)
         for kind in (2, 1, 3, 0):
-            send(near_copy(h, kind))
+            send(near_copy, h, kind)
 
     updated[...] = feats[...] + gain[...] * normed
     own_grad[...] = grad[...] + matmul_nt(g_pre, w_self[...])
-
-    def red_flow(q, direction, d):
-        return d < reach or direction == q and d == reach
 
     def red_hop(q, d):
         return 1 if q == 0 else (1 if d % 2 else 2)
@@ -362,7 +425,7 @@
 
     def add_arrived(total, h, q, direction, distances):
         for d in distances:
-            if red_flow(q, direction, d):
+            if in_flow(h, q, direction, d):
                 arrive(red_copy(h, q, direction, d))
                 total = total + red_in[ring_id(h, q, direction, d)].astype(F32)
         return total
@@ -370,12 +433,12 @@
     def red_sends(h, q, *distances):
         for d in distances:
             for direction in range(2):
-                if red_flow(q, direction, d):
+                if in_flow(h, q, direction, d):
                     total = messages[h, q, (d if direction == 0 else -d) % ring]
                     earlier = [d + 1] if q == 0 else ([3, 4] if d == 2 else [])
                     total = add_arrived(total, h, q, direction, earlier)
                     red_out[ring_id(h, q, direction, d)] = total.astype(BF16)
-                    send(red_copy(h, q, direction, d))
+                    send(red_copy, h, q, direction, d)
 
     def red_total(h, q):
         total = messages[h, q, 0]
@@ -395,7 +458,7 @@
 
     def swap_sends(h):
         swap_out[h] = red_total(h, 1).astype(BF16)
-        send(swap_copy(h))
+        send(swap_copy, h)
 
     def tile_gradient(t, carry):
         rel = jnp.clip(lax.rem(dest[0, t] - blk + HALO + blocks, blocks), 0, SPAN - 1)
@@ -411,28 +474,57 @@
     def tile_share(k):
         lax.fori_loop(k * share, (k + 1) * share, tile_gradient, 0, unroll=3 if share % 3 == 0 else 1)
 
-    for h in range(2):
+    def near_arrives(h):
         for kind in (1, 2):
             arrive(near_copy(h, kind, incoming=True))
-            send(near_copy(h, kind + 3))
+            send(near_copy, h, kind + 3)
         for kind in (0, 3, 4, 5):
             arrive(near_copy(h, kind, incoming=True))
-        make_messages(h, 1)
-        red_sends(h, 1, 4, 3)
-        make_messages(h, 0)
-        red_sends(h, 0, 4)
-        red_sends(h, 1, 1)
-    for h in range(2):
-        red_sends(h, 1, 2)
-        red_sends(h, 0, 3)
-    tile_share(0)
-    for h in range(2):
-        swap_sends(h)
-        red_sends(h, 0, 2)
-    tile_share(1)
-    for h in range(2):
-        red_sends(h, 0, 1)
-    tile_share(2)
+
+    first_sent = len(sent)
+
+    @pl.when(plane == 1)
+    def _():
+        for h in range(2):
+            near_arrives(h)
+            make_messages(h, 1)
+            red_sends(h, 1, 4, 3, 1)
+        for h in range(2):
+            red_sends(h, 1, 2)
+        for h in range(2):
+            make_messages(h, 0)
+        for h in range(2):
+            swap_sends(h)
+        for h in range(2):
+            red_sends(h, 0, 4)
+        for step in (3, 2, 1):
+            tile_share(3 - step)
+            for h in range(2):
+                red_sends(h, 0, step)
+
+    del sent[first_sent:]
+
+    @pl.when(plane == 0)
+    def _():
+        for h in range(2):
+            near_arrives(h)
+            make_messages(h, 1)
+            red_sends(h, 1, 4, 3)
+            make_messages(h, 0)
+            red_sends(h, 0, 4)
+            red_sends(h, 1, 1)
+        for h in range(2):
+            red_sends(h, 1, 2)
+            red_sends(h, 0, 3)
+        tile_share(0)
+        for h in range(2):
+            red_sends(h, 0, 2)
+            swap_sends(h)
+        tile_share(1)
+        for h in range(2):
+            red_sends(h, 0, 1)
+        tile_share(2)
+
     tile_share(3)
     for h in range(2):
         total = red_total(h, 0)
@@ -441,6 +533,9 @@
         at = slice(h * half, (h + 1) * half)
         grad_x[:, at] = own_grad[:, at] + total
 
+    for h in range(2):
+        pair_copy(h).wait_send()
+    ring_leaves()
     finish()
 
 
@@ -527,6 +622,7 @@
             dma((flows,)),
             dma((4,)),
             dma((4,)),
+            pltpu.SemaphoreType.REGULAR,
             dma((2 * SPAN,)),
             dma((2 * SPAN,)),
             dma((12,)),

time: 76.2 us -> 76 us (level)
  the two profiles are of different devices: /device:TPU:16 before, /device:TPU:512 now
where the time goes in v4:
time: 76 us; the launch traced here: 75.9 us
  Pallas kernels  74.6 us (98%)
  between operations  1.29 us (2%)
    pallas_call x1, Pallas kernels, body(): pl.pallas_call(kernel, out_shape=tuple((pltpu.VMEM(r.shape, r.dtype) for...  73.6 us

profile of v4, /device:TPU:512, one launch (start us, length us, event | category | flops | bytes accessed | tf_op | source)
XLA Modules:
  0.0 75.9 jit_solution(10946693165296425620)
XLA Ops:
  1.3 73.6 %shard_map.130 = (f32[128,256]{1,0:T(8,128)S(1)}, f32[128,256]{1,0:T(8,128)S(1)}, bf16[1,24,128,128]{3,2,1,0:T(8,128)(2,1)S(1)}) custom-call(s32[1,24]{1,0:T(1,128)} %dest_hbm.1, s32[1,24]{1,0:T(1,128)} %col_hbm.1, s32[1]{0:T(128)S(6)} %copy.14.count_hbm, f32[128,256]{1,0:T(8,128)} %feats_hbm.1, bf16[1,24,128,128]{3,2,1,0:T(8,128)(2,1)} %edge_hbm.1, ...), custom_call_target="tpu_custom_call" | custom-call | tf_op jit(solution)/shard_map/pallas_call | solution.py:584
  74.8 1.0 %shard_map.131 = (f32[128,256]{1,0:T(8,128)}, f32[128,256]{1,0:T(8,128)}, bf16[1,24,128,128]{3,2,1,0:T(8,128)(2,1)}) custom-call(f32[128,256]{1,0:T(8,128)S(1)} %get-tuple-element.6.refs_0_, f32[128,256]{1,0:T(8,128)S(1)} %get-tuple-element.7.refs_1_, bf16[1,24,128,128]{3,2,1,0:T(8,128)(2,1)S(1)} %get-tuple-element.8.refs_2_), custom_call_target="tpu_custom_call" | custom-call | tf_op jit(solution)/shard_map/pallas_call | solution.py:651

commit v5 on v3

--- a/solution.py
+++ b/solution.py
@@ -156,8 +156,8 @@
     def ring_id(h, q, direction, d):
         return ((h * 2 + q) * 2 + direction) * reach + d - 1
 
-    def in_flow(q, direction, d):
-        return d < reach or direction == q and d == reach
+    def in_flow(h, q, direction, d):
+        return d < reach or direction == (q + h) % 2 and d == reach
 
     def ring_copy(h, q, direction, d, incoming=False):
         sign = 1 if direction == 0 else -1
@@ -187,13 +187,13 @@
     def ring_sends(h, q, *distances):
         for d in distances:
             for direction in range(2):
-                if in_flow(q, direction, d):
+                if in_flow(h, q, direction, d):
                     send(ring_copy(h, q, direction, d))
 
     def ring_arrives(h, q, *distances):
         for d in distances:
             for direction in range(2):
-                if in_flow(q, direction, d):
+                if in_flow(h, q, direction, d):
                     arrive(ring_copy(h, q, direction, d, incoming=True))
 
     def ring_arrives_last(h):
@@ -337,9 +337,6 @@
     updated[...] = feats[...] + gain[...] * normed
     own_grad[...] = grad[...] + matmul_nt(g_pre, w_self[...])
 
-    def red_flow(q, direction, d):
-        return d < reach or direction == q and d == reach
-
     def red_hop(q, d):
         return 1 if q == 0 else (1 if d % 2 else 2)
 
@@ -362,7 +359,7 @@
 
     def add_arrived(total, h, q, direction, distances):
         for d in distances:
-            if red_flow(q, direction, d):
+            if in_flow(h, q, direction, d):
                 arrive(red_copy(h, q, direction, d))
                 total = total + red_in[ring_id(h, q, direction, d)].astype(F32)
         return total
@@ -370,7 +367,7 @@
     def red_sends(h, q, *distances):
         for d in distances:
             for direction in range(2):
-                if red_flow(q, direction, d):
+                if in_flow(h, q, direction, d):
                     total = messages[h, q, (d if direction == 0 else -d) % ring]
                     earlier = [d + 1] if q == 0 else ([3, 4] if d == 2 else [])
                     total = add_arrived(total, h, q, direction, earlier)
@@ -427,8 +424,8 @@
         red_sends(h, 0, 3)
     tile_share(0)
     for h in range(2):
+        red_sends(h, 0, 2)
         swap_sends(h)
-        red_sends(h, 0, 2)
     tile_share(1)
     for h in range(2):
         red_sends(h, 0, 1)

time: 76.2 us -> 76 us (level)
  the two profiles are of different devices: /device:TPU:16 before, /device:TPU:1 now
where the time goes in v5:
time: 76 us; the launch traced here: 75 us
  Pallas kernels  73.7 us (97%)
  between operations  1.29 us (2%)
    pallas_call x1, Pallas kernels, body(): pl.pallas_call(kernel, out_shape=tuple((pltpu.VMEM(r.shape, r.dtype) for...  72.7 us

profile of v5, /device:TPU:1, one launch (start us, length us, event | category | flops | bytes accessed | tf_op | source)
XLA Modules:
  0.0 75.0 jit_solution(15271407019902124167)
XLA Ops:
  1.3 72.7 %shard_map.130 = (f32[128,256]{1,0:T(8,128)S(1)}, f32[128,256]{1,0:T(8,128)S(1)}, bf16[1,24,128,128]{3,2,1,0:T(8,128)(2,1)S(1)}) custom-call(s32[1,24]{1,0:T(1,128)} %dest_hbm.1, s32[1,24]{1,0:T(1,128)} %col_hbm.1, s32[1]{0:T(128)S(6)} %copy.14.count_hbm, f32[128,256]{1,0:T(8,128)} %feats_hbm.1, bf16[1,24,128,128]{3,2,1,0:T(8,128)(2,1)} %edge_hbm.1, ...), custom_call_target="tpu_custom_call" | custom-call | tf_op jit(solution)/shard_map/pallas_call | solution.py:486
  74.0 1.0 %shard_map.131 = (f32[128,256]{1,0:T(8,128)}, f32[128,256]{1,0:T(8,128)}, bf16[1,24,128,128]{3,2,1,0:T(8,128)(2,1)}) custom-call(f32[128,256]{1,0:T(8,128)S(1)} %get-tuple-element.6.refs_0_, f32[128,256]{1,0:T(8,128)S(1)} %get-tuple-element.7.refs_1_, bf16[1,24,128,128]{3,2,1,0:T(8,128)(2,1)S(1)} %get-tuple-element.8.refs_2_), custom_call_target="tpu_custom_call" | custom-call | tf_op jit(solution)/shard_map/pallas_call | solution.py:552
